TPU v7x, 128 devices: a whole 4x4x4 slice. The times are simulated.
128 devices in a mesh: dp: 8 (over x, core), param: 16 (over z, y).
Axes of the slice: x: 4, y: 4, z: 4, core: 2. Of those that a mesh axis runs over, the one named last changes fastest.
Arguments:
- activations: bfloat16 [48, 2048, 8192], P('dp', None, 'param'), may hold values from -6 to 6
- output_gradient_rows: bfloat16 [48, 2048, 8192], P('dp', None, 'param'), may hold values from -0.19921875 to 0.19921875
- lengths: int32 [48], P('dp'), may hold values from 512 to 2048, as said below
- shrinking_factor: bfloat16 [8192, 128], P('param', 'dp'), may hold values from -0.0625 to 0.0625
- expanding_factor: bfloat16 [128, 8192], P('dp', 'param'), may hold values from -0.0625 to 0.0625
- shrinking_running_average: float32 [8192, 128], P('param', 'dp'), may hold values from -0.6 to 0.6
- shrinking_running_variance: float32 [8192, 128], P('param', 'dp'), may hold values from 0.01 to 1
- expanding_running_average: float32 [128, 8192], P('dp', 'param'), may hold values from -0.6 to 0.6
- expanding_running_variance: float32 [128, 8192], P('dp', 'param'), may hold values from 0.01 to 1
- up_rank_projector: float32 [128, 64], replicated
- up_width_projector: float32 [8192, 64], P('param'), may hold values from -0.0625 to 0.0625
- down_width_projector: float32 [8192, 64], P('param'), may hold values from -0.0625 to 0.0625
- down_rank_projector: float32 [128, 64], replicated
Outputs:
- features: float32 [48, 8192], P('dp', 'param')
Inputs may be any that keep to these rules, and one draw needn't show every extreme that they name: `lengths`: some example has 2048 valid tokens and some has 512.
All inputs are finite; a program needn't handle non-finite values.
Results may differ from a plain program's by a relative error of at most 0.00045.
Values may be sent and summed in bfloat16 or wider, within the bound.
No kernel may reach another device: no remote copies, remote signals or barrier semaphores. Data moves between devices by JAX's collectives and lax.ppermute only.
A program may use at most 128 MiB of HBM per device.

v0:
```python
import functools

import jax
import jax.numpy as jnp
from jax import lax
from jax.experimental import pallas as pl
from jax.experimental.pallas import tpu as pltpu
from jax.sharding import Mesh, PartitionSpec as P

BLK = 128
FOOT = 32
RES = 128.0
TOP = 32767.0
MIB = 1024 * 1024
VMEM = pltpu.VMEM
SMEM = pltpu.SMEM
F32 = jnp.float32
BF16 = jnp.bfloat16
I16 = jnp.int16
I32 = jnp.int32


def divisor(n):
    return next(c for c in (4, 3, 2, 1) if n % c == 0)


def scale_code(peak):
    return jnp.ceil(jnp.log(jnp.maximum(peak, 1e-30)) * (RES / 0.6931471805599453)) + 1.0


def scale_of(code):
    return jnp.exp2(code * (1.0 / RES))


def encode(x):
    code = scale_code(jnp.max(jnp.abs(x), axis=0, keepdims=True))
    q = jnp.round(x * (TOP / scale_of(code)))
    return q.astype(I32).astype(I16), code


def position():
    y, z = lax.axis_index("y").astype(I32), lax.axis_index("z").astype(I32)
    zero = lax.axis_index("core") == 0
    return jnp.where(zero, y, z), jnp.where(zero, z, y)


def block_counts(lens):
    return [(lens[e] + (BLK - 1)) // BLK for e in range(lens.shape[0])]


def locate(b, lens):
    n = lens.shape[0]
    start, e, end = jnp.int32(0), jnp.int32(0), jnp.int32(0)
    for count in block_counts(lens):
        end = end + count
        past = b >= end
        start = jnp.where(past, end, start)
        e = jnp.where(past, e + 1, e)
    inside = e < n
    e = jnp.minimum(e, n - 1)
    t = jnp.where(inside, (b - start) * BLK, 0)
    return e, t, jnp.where(inside, jnp.clip(lens[e] - t, 0, BLK), 0)


def dp_place():
    return lax.axis_index("x").astype(I32) * 2 + lax.axis_index("core").astype(I32)


def ring_of(x):
    n = 8
    others = [
        lax.ppermute(x, ("x", "core"), [(i, (i + s) % n) for i in range(n)]) for s in range(1, n)
    ]
    return [x] + others


def load_kernel(a_hbm, g_hbm, a, g, sems):
    copies = [
        pltpu.make_async_copy(a_hbm, a, sems.at[0]),
        pltpu.make_async_copy(g_hbm, g, sems.at[1]),
    ]
    for c in copies:
        c.start()
    for c in copies:
        c.wait()


def load(a, g):
    return pl.pallas_call(
        load_kernel,
        out_shape=[VMEM(a.shape, a.dtype), VMEM(g.shape, g.dtype)],
        in_specs=[pl.BlockSpec(memory_space=pl.ANY)] * 2,
        out_specs=[pl.BlockSpec(memory_space=VMEM)] * 2,
        scratch_shapes=[pltpu.SemaphoreType.DMA((2,))],
        compiler_params=pltpu.CompilerParams(vmem_limit_bytes=24 * MIB),
        cost_estimate=pl.CostEstimate(flops=0, bytes_accessed=a.size * 4, transcendentals=0),
    )(a, g)


def turn_kernel(*refs):
    parts, (w, flat) = refs[:8], refs[8:]
    me = dp_place()
    rank = parts[0].shape[1]
    for s, part in enumerate(parts):
        at = pl.ds(pl.multiple_of((me - s) % 8 * rank, rank), rank)
        for i in range(2):
            flat[i, at, :] = part[i]
    for i in range(2):
        w[i] = flat[i].T


def turn(parts):
    _, rank, width = parts[0].shape
    return pl.pallas_call(
        turn_kernel,
        out_shape=jax.ShapeDtypeStruct((2, width, 8 * rank), BF16),
        in_specs=[pl.BlockSpec(memory_space=VMEM)] * 8,
        out_specs=pl.BlockSpec(memory_space=VMEM),
        scratch_shapes=[VMEM((2, 8 * rank, width), BF16)],
        compiler_params=pltpu.CompilerParams(vmem_limit_bytes=2 * MIB),
    )(*parts)


def foot(ref, start, codes, count):
    rows = [codes[k] for k in range(count)]
    rows.append(jnp.zeros((FOOT - count, 256), F32))
    ref[start:, :] = jnp.concatenate(rows, axis=0).astype(I32).astype(I16)


def partial_kernel(nblk, s, lens, w, a, g, q, codes):
    first = (position()[0] + s) % 4 * nblk

    def block(k, carry):
        e, t, count = locate(first + k, lens)
        t = pl.multiple_of(t, BLK)
        at = pl.ds(pl.multiple_of(k * BLK, BLK), BLK)
        live = lax.broadcasted_iota(I32, (BLK, 128), 0) < count
        for i, rows in enumerate((a, g)):
            x = jnp.dot(rows[e, pl.ds(t, BLK), :], w[i], preferred_element_type=F32)
            x = jnp.where(live, x, 0.0)
            coded, code = encode(x)
            q[at, i * 128 : (i + 1) * 128] = coded
            codes[k, :, i * 128 : (i + 1) * 128] = code
        return carry

    lax.fori_loop(0, nblk, block, 0, unroll=divisor(nblk))
    foot(q, nblk * BLK, codes, nblk)


def partial_piece(lens, w, a, g, nblk, s):
    rows = nblk * BLK
    return pl.pallas_call(
        functools.partial(partial_kernel, nblk, s),
        out_shape=jax.ShapeDtypeStruct((rows + FOOT, 256), I16),
        in_specs=[pl.BlockSpec(memory_space=SMEM)] + [pl.BlockSpec(memory_space=VMEM)] * 3,
        out_specs=pl.BlockSpec(memory_space=VMEM),
        scratch_shapes=[VMEM((FOOT, 1, 256), F32)],
        compiler_params=pltpu.CompilerParams(vmem_limit_bytes=2 * MIB),
        cost_estimate=pl.CostEstimate(
            flops=1000, bytes_accessed=1000, transcendentals=0
        ),
    )(lens, w, a, g)


def far_kernel(nblk, chunk, s, lens, w, a_hbm, g_hbm, q, a, g, codes, sems):
    first = (position()[0] + s) % 4 * nblk

    def copies(k):
        e, t, _ = locate(first + k, lens)
        here = pl.ds(pl.multiple_of(k * BLK, BLK), BLK)
        there = pl.ds(pl.multiple_of(t, BLK), BLK)
        return (
            pltpu.make_async_copy(a_hbm.at[e, there], a.at[here], sems.at[0, k]),
            pltpu.make_async_copy(g_hbm.at[e, there], g.at[here], sems.at[1, k]),
        )

    def begin(k, carry):
        for c in copies(k):
            c.start()
        return carry

    lax.fori_loop(0, nblk, begin, 0)

    def some(j, carry):
        for k in range(chunk):
            for c in copies(j * chunk + k):
                c.wait()
        at = pl.ds(pl.multiple_of(j * (chunk * BLK), BLK), chunk * BLK)
        for i, rows in enumerate((a, g)):
            x = jnp.dot(rows[at, :], w[i], preferred_element_type=F32)
            for k in range(chunk):
                b = j * chunk + k
                live = lax.broadcasted_iota(I32, (BLK, 128), 0) < locate(first + b, lens)[2]
                coded, code = encode(jnp.where(live, x[k * BLK : (k + 1) * BLK], 0.0))
                q[pl.ds(pl.multiple_of(b * BLK, BLK), BLK), i * 128 : (i + 1) * 128] = coded
                codes[b, :, i * 128 : (i + 1) * 128] = code
        return carry

    lax.fori_loop(0, nblk // chunk, some, 0)
    foot(q, nblk * BLK, codes, nblk)


def far_piece(lens, w, a, g, nblk, s):
    rows = nblk * BLK
    chunk = 2 if nblk % 2 == 0 else 1
    return pl.pallas_call(
        functools.partial(far_kernel, nblk, chunk, s),
        out_shape=jax.ShapeDtypeStruct((rows + FOOT, 256), I16),
        in_specs=[pl.BlockSpec(memory_space=SMEM), pl.BlockSpec(memory_space=VMEM)]
        + [pl.BlockSpec(memory_space=pl.ANY)] * 2,
        out_specs=pl.BlockSpec(memory_space=VMEM),
        scratch_shapes=[
            VMEM((rows, a.shape[2]), BF16),
            VMEM((rows, a.shape[2]), BF16),
            VMEM((FOOT, 1, 256), F32),
            pltpu.SemaphoreType.DMA((2, nblk)),
        ],
        compiler_params=pltpu.CompilerParams(vmem_limit_bytes=50 * MIB),
        cost_estimate=pl.CostEstimate(flops=1000, bytes_accessed=1000, transcendentals=0),
    )(lens, w, a, g)


def scales_of(refs, rows, count):
    return [scale_of(r[rows:, :].astype(I32).astype(F32)) * (1.0 / TOP) for r in refs]


def value(ref, start, n):
    return ref[pl.ds(start, n), :].astype(I32).astype(F32)


def middle_kernel(rows, sub, step, which, q0, q1, q2, q3, *rest):
    refs, outs, (scales, codes) = (q0, q1, q2, q3), rest[:-2], rest[-2:]
    two = position()[1]
    for i, s in enumerate(scales_of(refs, rows, rows // BLK)):
        scales[i] = s
    for s, out in zip(which, outs):
        begin = (two + s) % 4 * sub

        def some(j, carry, out=out, begin=begin):
            at = pl.multiple_of(begin + j * step, step)
            total = None
            for i, r in enumerate(refs):
                v = value(r, at, step) * scales[i, pl.ds(at // BLK, 1), :]
                total = v if total is None else total + v
            coded, code = encode(total)
            out[pl.ds(pl.multiple_of(j * step, step), step), :] = coded
            codes[j] = code
            return carry

        lax.fori_loop(0, sub // step, some, 0, unroll=divisor(sub // step))
        foot(out, sub, codes, sub // step)


def middle_sum(pieces, rows, sub, step, which):
    return pl.pallas_call(
        functools.partial(middle_kernel, rows, sub, step, which),
        out_shape=[jax.ShapeDtypeStruct((sub + FOOT, 256), I16)] * len(which),
        in_specs=[pl.BlockSpec(memory_space=VMEM)] * 4,
        out_specs=[pl.BlockSpec(memory_space=VMEM)] * len(which),
        scratch_shapes=[VMEM((4, FOOT, 256), F32), VMEM((FOOT, 1, 256), F32)],
        compiler_params=pltpu.CompilerParams(vmem_limit_bytes=4 * MIB),
        cost_estimate=pl.CostEstimate(
            flops=rows * 64 * 8 * len(which), bytes_accessed=rows * 256 * 2, transcendentals=0
        ),
    )(*pieces)


def last_kernel(sub, step, r0, r1, r2, r3, out):
    refs = (r0, r1, r2, r3)
    scales = scales_of(refs, sub, sub // step)
    for j in range(sub // step):
        total = None
        for i, r in enumerate(refs):
            v = value(r, j * step, step) * scales[i][j : j + 1, :]
            total = v if total is None else total + v
        out[j * step : (j + 1) * step, :] = total.astype(BF16)


def last_sum(pieces, sub, step):
    return pl.pallas_call(
        functools.partial(last_kernel, sub, step),
        out_shape=jax.ShapeDtypeStruct((sub, 256), BF16),
        in_specs=[pl.BlockSpec(memory_space=VMEM)] * 4,
        out_specs=pl.BlockSpec(memory_space=VMEM),
        compiler_params=pltpu.CompilerParams(vmem_limit_bytes=3 * MIB),
        cost_estimate=pl.CostEstimate(
            flops=sub * 256 * 8, bytes_accessed=sub * 256 * 10, transcendentals=0
        ),
    )(*pieces)


def precondition(grad, first, second):
    return (first + 0.1 * grad) / (jnp.sqrt(second + 0.001 * grad * grad) + 1e-08)


def join_kernel(r0, r1, r2, r3, out):
    two = position()[1]
    for s, r in enumerate((r0, r1, r2, r3)):
        out[(two - s) % 4] = r[...]


def join(parts):
    sub = parts[0].shape[0]
    return pl.pallas_call(
        join_kernel,
        out_shape=jax.ShapeDtypeStruct((4, sub, 256), BF16),
        in_specs=[pl.BlockSpec(memory_space=VMEM)] * 4,
        out_specs=pl.BlockSpec(memory_space=VMEM),
        compiler_params=pltpu.CompilerParams(vmem_limit_bytes=2 * MIB),
    )(*parts).reshape(4 * sub, 256)


def gather_sums(which, nblk, lens, pieces, a, g, up, down):
    tn = (((0,), (0,)), ((), ()))
    one = position()[0]
    for s, piece in zip(which, pieces):
        low = (one - s) % 4 * nblk

        def example(e, begin, piece=piece, low=low):
            count = (lens[e] + (BLK - 1)) // BLK
            first = jnp.clip(begin - low, 0, nblk)
            some = jnp.clip(begin + count - low, 0, nblk) - first
            skip = jnp.maximum(low - begin, 0)

            def add(b, n):
                packed = pl.ds(pl.multiple_of((first + b) * BLK, BLK), n * BLK)
                rows = pl.ds(pl.multiple_of((skip + b) * BLK, BLK), n * BLK)
                up[e] += lax.dot_general(
                    piece[packed, :128], g[e, rows, :], tn, preferred_element_type=F32
                )
                down[e] += lax.dot_general(
                    piece[packed, 128:], a[e, rows, :], tn, preferred_element_type=F32
                )

            def eight(i, carry):
                add(i * 8, 8)
                return carry

            lax.fori_loop(0, some // 8, eight, 0)
            for n in (4, 2, 1):

                @pl.when((some // n) % 2 == 1)
                def _(n=n):
                    add(some // (2 * n) * (2 * n), n)

            return begin + count

        lax.fori_loop(0, 6, example, jnp.int32(0))


def two_parts(x):
    big = x.astype(BF16)
    return big, (x - big.astype(F32)).astype(BF16)


def final_kernel(which, nblk, lens, *refs):
    n = len(which)
    a, g = refs[n : n + 2]
    parts = refs[n + 2 : n + 10]
    urp, uwp, dwp, drp, out, up, down, moments, wide2 = refs[n + 10 :]
    nt = (((1,), (1,)), ((), ()))
    me = dp_place()
    rank = parts[0].shape[0] // 4
    for s, part in enumerate(parts):
        at = pl.ds(pl.multiple_of((me - s) % 8 * rank, rank), rank)
        for i in range(4):
            moments[i, at, :] = part[i * rank : (i + 1) * rank, :] * (0.9, 0.999)[i % 2]
    up[...] = jnp.zeros_like(up)
    down[...] = jnp.zeros_like(down)
    gather_sums(which, nblk, lens, refs[:n], a, g, up, down)

    sides = []
    for i, (width, side) in enumerate(((uwp, urp), (dwp, drp))):
        big, rest = two_parts(width[...])
        wide2[i, :64, :] = big
        wide2[i, 64:, :] = rest
        sides.append(side[...])

    def examples(j, carry):
        for i, grad in enumerate((up, down)):
            pre = jnp.concatenate(
                [
                    precondition(grad[2 * j + k], moments[2 * i], moments[2 * i + 1])
                    for k in range(2)
                ],
                axis=0,
            )
            big, rest = two_parts(pre)
            both = lax.dot_general(big, wide2[i], nt, preferred_element_type=F32)
            wide = both[:, :64] + (
                both[:, 64:]
                + lax.dot_general(rest, wide2[i, :64, :], nt, preferred_element_type=F32)
            )
            for k in range(2):
                out[2 * j + k, i * 64 : (i + 1) * 64, :] = jnp.dot(
                    sides[i],
                    wide[k * 128 : (k + 1) * 128],
                    precision=lax.Precision.HIGHEST,
                    preferred_element_type=F32,
                )
        return carry

    lax.fori_loop(0, 3, examples, 0)


def final_grads(which, nblk, lens, pieces, a, g, moments, *projectors):
    return pl.pallas_call(
        functools.partial(final_kernel, which, nblk),
        out_shape=jax.ShapeDtypeStruct((6, 128, 64), F32),
        in_specs=[pl.BlockSpec(memory_space=SMEM)]
        + [pl.BlockSpec(memory_space=VMEM)] * (len(which) + 14),
        out_specs=pl.BlockSpec(memory_space=VMEM),
        scratch_shapes=[
            VMEM((6, 128, 512), F32),
            VMEM((6, 128, 512), F32),
            VMEM((4, 128, 512), F32),
            VMEM((2, 128, 512), BF16),
        ],
        compiler_params=pltpu.CompilerParams(vmem_limit_bytes=6 * MIB),
        cost_estimate=pl.CostEstimate(
            flops=4 * nblk * len(which) * BLK * 512 * 128,
            bytes_accessed=nblk * len(which) * BLK * 512,
            transcendentals=0,
        ),
    )(lens, *pieces, a, g, *moments, *projectors)


def shifts(first, s):
    pairs = []
    for core in range(2):
        for z in range(4):
            for y in range(4):
                along_y = (core == 0) == first
                to = (z, (y + s) % 4) if along_y else ((z + s) % 4, y)
                pairs.append((core * 16 + z * 4 + y, core * 16 + to[0] * 4 + to[1]))
    return pairs


def send(x, first, s):
    return x if s == 0 else lax.ppermute(x, ("core", "z", "y"), shifts(first, s))


def features(nb, lens, w, moments, a, g, projectors):
    rows, sub, step, per = nb * BLK // 4, nb * BLK // 16, 32, nb // 4
    got = [None] * 4
    coded = far_piece(lens, w, a, g, per, 2)
    got[2] = send(coded, True, 2)
    coded, a, g = lax.optimization_barrier((coded, a, g))
    a, g = load(a, g)
    for s in (1, 3):
        got[s] = send(partial_piece(lens, w, a, g, per, s), True, s)
    got[2], own_lens = lax.optimization_barrier((got[2], lens))
    got[0] = partial_piece(own_lens, w, a, g, per, 0)
    got[0], moments = lax.optimization_barrier((got[0], moments))
    ring = ring_of(moments)
    back = [None] * 4
    for which in ((2,), (1, 3, 0)):
        for s, mid in zip(which, middle_sum(got, rows, sub, step, which)):
            back[s] = send(mid, False, s)
    own = last_sum(back, sub, step)
    piece = join([send(own, False, s) for s in range(4)])
    pieces = {s: send(piece, True, s) for s in (0, 1, 3, 2)}
    which = (0, 1, 3, 2)
    return final_grads(which, per, lens, [pieces[s] for s in which], a, g, ring, *projectors)


def share(x, axes, n):
    return lax.all_to_all(jnp.broadcast_to(x[None], (n,) + x.shape), axes, 0, 0, tiled=True)


def length_rows(lengths, rank, width):
    rows = jnp.stack([lengths // 64, lengths % 64])
    return jnp.pad(rows, ((0, rank - 2), (0, width - lengths.shape[0]))).astype(BF16)


def blocks_needed(rows, n):
    pairs = jnp.stack([r[2, :2, :n] for r in rows]).astype(F32)
    lengths = (pairs[:, 0] * 64.0 + pairs[:, 1]).astype(I32)
    return jnp.max(jnp.sum((lengths + (BLK - 1)) // BLK, axis=1))


def body(a, g, lengths, sf, ef, sra, srv, era, erv, urp, uwp, dwp, drp):
    param = ("z", "y")
    mine = jnp.stack([sf.T, ef, length_rows(lengths, sf.shape[1], sf.shape[0])])
    rows = ring_of(mine)
    w = turn(rows)
    moments = jnp.concatenate([era, erv, sra.T, srv.T], axis=0)
    projectors = (urp.T, uwp.T, dwp.T, drp.T)
    most = a.shape[0] * a.shape[1] // BLK
    sizes = [80, most]
    need = blocks_needed(rows, lengths.shape[0])
    which = sum((need > nb).astype(I32) for nb in sizes[:-1])
    part = lax.switch(
        which,
        [functools.partial(features, nb) for nb in sizes],
        lengths,
        w,
        moments,
        a,
        g,
        projectors,
    )
    owned = jnp.swapaxes(part.reshape(6, 16, 8, 64), 0, 1)
    raw = jnp.sum(lax.all_to_all(owned, param, 0, 0, tiled=True), axis=0)
    square = jnp.sum(raw * raw, axis=(1, 2))
    square = share(jnp.broadcast_to(square[:, None], (6, 128)), param, 16)
    scale = lax.rsqrt(jnp.sum(square, axis=0)[:, 0] / 8192.0 + 1e-06)
    return (raw * scale[:, None, None]).reshape(6, 512)


def solution(mesh):
    grid = Mesh(mesh.devices.reshape(4, 2, 4, 4), ("x", "core", "z", "y"))
    dp, param = ("x", "core"), ("z", "y")
    in_specs = (
        P(dp, None, param),
        P(dp, None, param),
        P(dp),
        P(param, dp),
        P(dp, param),
        P(param, dp),
        P(param, dp),
        P(dp, param),
        P(dp, param),
        P(),
        P(param, None),
        P(param, None),
        P(),
    )
    return jax.shard_map(body, mesh=grid, in_specs=in_specs, out_specs=P(dp, param), check_vma=False)
```

profile of v0, /device:TPU:6, one launch (start us, length us, event | category | flops | bytes accessed | tf_op | source)
XLA Modules:
  0.0 159.6 jit_solution(5981794200468545602)
XLA Ops:
  1.9 2.4 %collective-permute-start.40 = (bf16[3,16,512]{2,1,0:T(8,128)(2,1)S(1)}, bf16[3,16,512]{2,1,0:T(8,128)(2,1)S(1)}, u32[]{:S(2)}, u32[]{:S(2)}) collective-permute-start(bf16[3,16,512]{2,1,0:T(8,128)(2,1)S(1)} %pad_maximum_fusion.1.refs_0_), channel_id=1, source_target_pairs={{0,48},{16,64},{32,80},{48,96},{64,112},{80,0},{96,16},{112,32},{1... | collective-permute-start | bytes 147464 | tf_op jit(solution)/shard_map/ppermute | solution.py:72
  11.0 2.6 %collective-permute-done.43.refs_6_ = bf16[3,16,512]{2,1,0:T(8,128)(2,1)S(1)} collective-permute-done((bf16[3,16,512]{2,1,0:T(8,128)(2,1)S(1)}, bf16[3,16,512]{2,1,0:T(8,128)(2,1)S(1)}, u32[]{:S(2)}, u32[]{:S(2)}) %collective-permute-start.43) | collective-permute-done | bytes 49184 | tf_op jit(solution)/shard_map/ppermute | solution.py:72
  15.2 117.6 %conditional.1 = (f32[6,128,64]{2,1,0:T(8,128)S(1)}) conditional(s32[]{:T(128)} %clamp.3, (s32[6]{0:T(128)}, bf16[2,512,128]{2,1,0:T(8,128)(2,1)S(1)}, bf16[6,2048,512]{2,1,0:T(8,128)(2,1)}, bf16[6,2048,512]{2,1,0:T(8,128)(2,1)}, f32[64,512]{1,0:T(8,128)S(1)}, /*index=5*/f32[64,128]{1,0:T(8,128)}, f32[64,512]{1,0:T(8,128)}, f32[64,512]{1,0:T(8,128)}, ...), branch_computations={%region_2.3_spmd, %region_3.4_spmd} | conditional | flops 3229093888 | bytes 240128960 | solution.py:493
  15.2 6.1 %branch_0_fun.10 = s16[2592,256]{1,0:T(8,128)(2,1)S(1)} custom-call(s32[6]{0:T(128)} %get-tuple-element.48.lens, bf16[2,512,128]{2,1,0:T(8,128)(2,1)S(1)} %get-tuple-element.45.w, bf16[6,2048,512]{2,1,0:T(8,128)(2,1)} %get-tuple-element.49.a_hbm, bf16[6,2048,512]{2,1,0:T(8,128)(2,1)} %get-tuple-element.50.g_hbm), custom_call_target="tpu_custom_call" | custom-call | flops 1000 | bytes 1000 | tf_op jit(solution)/shard_map/cond/branch_0_fun/pallas_call | solution.py:206
  21.3 3.3 %collective-permute-start = (s16[2592,256]{1,0:T(8,128)(2,1)S(1)}, s16[2592,256]{1,0:T(8,128)(2,1)S(1)}, u32[]{:S(2)}, u32[]{:S(2)}) collective-permute-start(s16[2592,256]{1,0:T(8,128)(2,1)S(1)} %branch_0_fun.10), channel_id=1, source_target_pairs={{0,2},{1,3},{2,0},{3,1},{4,6},{5,7},{6,4},{7,5},{8,10},{9,11},{10,... | collective-permute-start | bytes 3981320 | tf_op jit(solution)/shard_map/cond/branch_0_fun/ppermute | solution.py:440
  24.6 5.4 %branch_0_fun.11 = (bf16[6,2048,512]{2,1,0:T(8,128)(2,1)S(1)}, bf16[6,2048,512]{2,1,0:T(8,128)(2,1)S(1)}) custom-call(bf16[6,2048,512]{2,1,0:T(8,128)(2,1)S(1)} %copy-done.2, bf16[6,2048,512]{2,1,0:T(8,128)(2,1)} %get-tuple-element.50.g_hbm), custom_call_target="tpu_custom_call" | custom-call | bytes 25165824 | tf_op jit(solution)/shard_map/cond/branch_0_fun/pallas_call | solution.py:89
  30.0 3.1 %branch_0_fun.14 = s16[2592,256]{1,0:T(8,128)(2,1)S(1)} custom-call(s32[6]{0:T(128)S(1)} %copy-done.12, bf16[2,512,128]{2,1,0:T(8,128)(2,1)S(1)} %get-tuple-element.45.w, bf16[6,2048,512]{2,1,0:T(8,128)(2,1)S(1)} %get-tuple-element.51.a.refs_4_, bf16[6,2048,512]{2,1,0:T(8,128)(2,1)S(1)} %get-tuple-element.52.g.refs_5_), custom_call_target="tpu_custom_call" | custom-call | flops 1000 | bytes 1000 | tf_op jit(solution)/shard_map/cond/branch_0_fun/pallas_call | solution.py:152
  34.4 3.1 %branch_0_fun.13 = s16[2592,256]{1,0:T(8,128)(2,1)S(1)} custom-call(s32[6]{0:T(128)S(1)} %copy-done.12, bf16[2,512,128]{2,1,0:T(8,128)(2,1)S(1)} %get-tuple-element.45.w, bf16[6,2048,512]{2,1,0:T(8,128)(2,1)S(1)} %get-tuple-element.51.a.refs_4_, bf16[6,2048,512]{2,1,0:T(8,128)(2,1)S(1)} %get-tuple-element.52.g.refs_5_), custom_call_target="tpu_custom_call" | custom-call | flops 1000 | bytes 1000 | tf_op jit(solution)/shard_map/cond/branch_0_fun/pallas_call | solution.py:152
  40.7 3.1 %branch_0_fun.12.q0 = s16[2592,256]{1,0:T(8,128)(2,1)S(1)} custom-call(s32[6]{0:T(128)S(1)} %copy-done.12, bf16[2,512,128]{2,1,0:T(8,128)(2,1)S(1)} %get-tuple-element.45.w, bf16[6,2048,512]{2,1,0:T(8,128)(2,1)S(1)} %get-tuple-element.51.a.refs_4_, bf16[6,2048,512]{2,1,0:T(8,128)(2,1)S(1)} %get-tuple-element.52.g.refs_5_), custom_call_target="tpu_custom_call" | custom-call | flops 1000 | bytes 1000 | tf_op jit(solution)/shard_map/cond/branch_0_fun/pallas_call | solution.py:152
  43.7 11.5 %collective-permute-done.2.q3 = s16[2592,256]{1,0:T(8,128)(2,1)S(1)} collective-permute-done((s16[2592,256]{1,0:T(8,128)(2,1)S(1)}, s16[2592,256]{1,0:T(8,128)(2,1)S(1)}, u32[]{:S(2)}, u32[]{:S(2)}) %collective-permute-start.2) | collective-permute-done | bytes 1327136 | tf_op jit(solution)/shard_map/cond/branch_0_fun/ppermute | solution.py:440
  57.2 4.0 %collective-permute-start.4 = (s16[672,256]{1,0:T(8,128)(2,1)S(1)}, s16[672,256]{1,0:T(8,128)(2,1)S(1)}, u32[]{:S(2)}, u32[]{:S(2)}) collective-permute-start(s16[672,256]{1,0:T(8,128)(2,1)S(1)} %branch_0_fun.16), channel_id=1, source_target_pairs={{0,8},{1,9},{2,10},{3,11},{4,12},{5,13},{6,14},{7,15},{8,0},{9,1},... | collective-permute-start | bytes 1032200 | tf_op jit(solution)/shard_map/cond/branch_0_fun/ppermute | solution.py:440
  66.4 5.2 %collective-permute-done.3.r1 = s16[672,256]{1,0:T(8,128)(2,1)S(1)} collective-permute-done((s16[672,256]{1,0:T(8,128)(2,1)S(1)}, s16[672,256]{1,0:T(8,128)(2,1)S(1)}, u32[]{:S(2)}, u32[]{:S(2)}) %collective-permute-start.3) | collective-permute-done | bytes 344096 | tf_op jit(solution)/shard_map/cond/branch_0_fun/ppermute | solution.py:440
  72.6 4.2 %collective-permute-start.7 = (bf16[640,256]{1,0:T(8,128)(2,1)S(1)}, bf16[640,256]{1,0:T(8,128)(2,1)S(1)}, u32[]{:S(2)}, u32[]{:S(2)}) collective-permute-start(bf16[640,256]{1,0:T(8,128)(2,1)S(1)} %branch_0_fun.17.r0), channel_id=1, source_target_pairs={{0,8},{1,9},{2,10},{3,11},{4,12},{5,13},{6,14},{7,15},{8,0},{9,1},... | collective-permute-start | bytes 983048 | tf_op jit(solution)/shard_map/cond/branch_0_fun/ppermute | solution.py:440
  76.8 3.6 %collective-permute-done.6.r1 = bf16[640,256]{1,0:T(8,128)(2,1)S(1)} collective-permute-done((bf16[640,256]{1,0:T(8,128)(2,1)S(1)}, bf16[640,256]{1,0:T(8,128)(2,1)S(1)}, u32[]{:S(2)}, u32[]{:S(2)}) %collective-permute-start.6) | collective-permute-done | bytes 327712 | tf_op jit(solution)/shard_map/cond/branch_0_fun/ppermute | solution.py:440
  80.4 5.0 %collective-permute-done.7.r2 = bf16[640,256]{1,0:T(8,128)(2,1)S(1)} collective-permute-done((bf16[640,256]{1,0:T(8,128)(2,1)S(1)}, bf16[640,256]{1,0:T(8,128)(2,1)S(1)}, u32[]{:S(2)}, u32[]{:S(2)}) %collective-permute-start.7) | collective-permute-done | bytes 327712 | tf_op jit(solution)/shard_map/cond/branch_0_fun/ppermute | solution.py:440
  89.2 4.6 %collective-permute-done.12.refs_7_ = f32[64,512]{1,0:T(8,128)S(1)} collective-permute-done((f32[64,512]{1,0:T(8,128)S(1)}, f32[64,512]{1,0:T(8,128)S(1)}, u32[]{:S(2)}, u32[]{:S(2)}) %collective-permute-start.12) | collective-permute-done | bytes 131104 | tf_op jit(solution)/shard_map/cond/branch_0_fun/ppermute | solution.py:72
  95.4 4.4 %collective-permute-done.14.refs_9_ = f32[64,512]{1,0:T(8,128)S(1)} collective-permute-done((f32[64,512]{1,0:T(8,128)S(1)}, f32[64,512]{1,0:T(8,128)S(1)}, u32[]{:S(2)}, u32[]{:S(2)}) %collective-permute-start.14) | collective-permute-done | bytes 131104 | tf_op jit(solution)/shard_map/cond/branch_0_fun/ppermute | solution.py:72
  102.4 3.2 %collective-permute-done.16.refs_11_ = f32[64,512]{1,0:T(8,128)S(1)} collective-permute-done((f32[64,512]{1,0:T(8,128)S(1)}, f32[64,512]{1,0:T(8,128)S(1)}, u32[]{:S(2)}, u32[]{:S(2)}) %collective-permute-start.16) | collective-permute-done | bytes 131104 | tf_op jit(solution)/shard_map/cond/branch_0_fun/ppermute | solution.py:72
  105.6 4.3 %collective-permute-done.17.refs_12_ = f32[64,512]{1,0:T(8,128)S(1)} collective-permute-done((f32[64,512]{1,0:T(8,128)S(1)}, f32[64,512]{1,0:T(8,128)S(1)}, u32[]{:S(2)}, u32[]{:S(2)}) %collective-permute-start.17) | collective-permute-done | bytes 131104 | tf_op jit(solution)/shard_map/cond/branch_0_fun/ppermute | solution.py:72
  110.0 10.1 %collective-permute-done.9.refs_1_ = bf16[2560,256]{1,0:T(8,128)(2,1)S(1)} collective-permute-done((bf16[2560,256]{1,0:T(8,128)(2,1)S(1)}, bf16[2560,256]{1,0:T(8,128)(2,1)S(1)}, u32[]{:S(2)}, u32[]{:S(2)}) %collective-permute-start.9) | collective-permute-done | bytes 1310752 | tf_op jit(solution)/shard_map/cond/branch_0_fun/ppermute | solution.py:440
  120.1 12.2 %branch_0_fun.19 = f32[6,128,64]{2,1,0:T(8,128)S(1)} custom-call(s32[6]{0:T(128)S(1)} %copy-done.12, bf16[2560,256]{1,0:T(8,128)(2,1)S(1)} %bitcast.29, bf16[2560,256]{1,0:T(8,128)(2,1)S(1)} %collective-permute-done.9.refs_1_, bf16[2560,256]{1,0:T(8,128)(2,1)S(1)} %collective-permute-done.10.refs_2_, bf16[2560,256]{1,0:T(8,128)(2,1)S(1)} %collective-permute-done.11.refs_3_, ...), custom_call_target="tpu_custom_call" | custom-call | flops 2684354560 | bytes 5242880 | tf_op jit(solution)/shard_map/cond/branch_0_fun/pallas_call | solution.py:407
  133.1 11.9 %all_to_all.10 = f32[16,1,3072]{2,1,0:T(1,128)S(1)} all-to-all(f32[16,1,3072]{2,1,0:T(1,128)S(1)} %reshape.31), channel_id=1, replica_groups=mesh['x'=4,'core'=2,'z'=4,'y'=4] {'z','y'}, dimensions={0} | all-to-all | bytes 393216 | tf_op jit(solution)/shard_map/all_to_all | solution.py:504
  147.6 3.5 %all-to-all-start.1 = ((f32[16,6,128]{2,1,0:T(8,128)}), f32[16,6,128]{2,1,0:T(8,128)S(1)}, u32[]{:S(2)}, u32[]{:S(2)}) async-start(f32[16,6,128]{2,1,0:T(8,128)} %broadcast_in_dim_broadcast_in_dim_broadcast_in_dim.2), calls=%async_computation.1 | async-start | bytes 131072 | tf_op jit(solution)/shard_map/all_to_all | solution.py:468
  151.2 7.5 %all-to-all-done.1 = f32[16,6,128]{2,1,0:T(8,128)S(1)} async-done(((f32[16,6,128]{2,1,0:T(8,128)}), f32[16,6,128]{2,1,0:T(8,128)S(1)}, u32[]{:S(2)}, u32[]{:S(2)}) %all-to-all-start.1) | async-done | bytes 49184 | tf_op jit(solution)/shard_map/all_to_all | solution.py:468
  (83 shorter events, 33.9 us)
Async XLA Ops:
  1.4 6.8 %collective-permute-start.38 = (bf16[3,16,512]{2,1,0:T(8,128)(2,1)S(1)}, bf16[3,16,512]{2,1,0:T(8,128)(2,1)S(1)}, u32[]{:S(2)}, u32[]{:S(2)}) collective-permute-start(bf16[3,16,512]{2,1,0:T(8,128)(2,1)S(1)} %pad_maximum_fusion.1.refs_0_), channel_id=1, source_target_pairs={{0,16},{16,32},{32,48},{48,64},{64,80},{80,96},{96,112},{112,0},{1... | collective-permute-start | bytes 147464 | tf_op jit(solution)/shard_map/ppermute | solution.py:72
  1.4 6.9 %collective-permute-start.39 = (bf16[3,16,512]{2,1,0:T(8,128)(2,1)S(1)}, bf16[3,16,512]{2,1,0:T(8,128)(2,1)S(1)}, u32[]{:S(2)}, u32[]{:S(2)}) collective-permute-start(bf16[3,16,512]{2,1,0:T(8,128)(2,1)S(1)} %pad_maximum_fusion.1.refs_0_), channel_id=1, source_target_pairs={{0,32},{16,48},{32,64},{48,80},{64,96},{80,112},{96,0},{112,16},{1... | collective-permute-start | bytes 147464 | tf_op jit(solution)/shard_map/ppermute | solution.py:72
  1.9 7.4 %collective-permute-start.40 = (bf16[3,16,512]{2,1,0:T(8,128)(2,1)S(1)}, bf16[3,16,512]{2,1,0:T(8,128)(2,1)S(1)}, u32[]{:S(2)}, u32[]{:S(2)}) collective-permute-start(bf16[3,16,512]{2,1,0:T(8,128)(2,1)S(1)} %pad_maximum_fusion.1.refs_0_), channel_id=1, source_target_pairs={{0,48},{16,64},{32,80},{48,96},{64,112},{80,0},{96,16},{112,32},{1... | collective-permute-start | bytes 147464 | tf_op jit(solution)/shard_map/ppermute | solution.py:72
  4.3 5.6 %collective-permute-start.41 = (bf16[3,16,512]{2,1,0:T(8,128)(2,1)S(1)}, bf16[3,16,512]{2,1,0:T(8,128)(2,1)S(1)}, u32[]{:S(2)}, u32[]{:S(2)}) collective-permute-start(bf16[3,16,512]{2,1,0:T(8,128)(2,1)S(1)} %pad_maximum_fusion.1.refs_0_), channel_id=1, source_target_pairs={{0,64},{16,80},{32,96},{48,112},{64,0},{80,16},{96,32},{112,48},{1... | collective-permute-start | bytes 147464 | tf_op jit(solution)/shard_map/ppermute | solution.py:72
  5.4 5.6 %collective-permute-start.42 = (bf16[3,16,512]{2,1,0:T(8,128)(2,1)S(1)}, bf16[3,16,512]{2,1,0:T(8,128)(2,1)S(1)}, u32[]{:S(2)}, u32[]{:S(2)}) collective-permute-start(bf16[3,16,512]{2,1,0:T(8,128)(2,1)S(1)} %pad_maximum_fusion.1.refs_0_), channel_id=1, source_target_pairs={{0,80},{16,96},{32,112},{48,0},{64,16},{80,32},{96,48},{112,64},{1... | collective-permute-start | bytes 147464 | tf_op jit(solution)/shard_map/ppermute | solution.py:72
  8.2 5.4 %collective-permute-start.43 = (bf16[3,16,512]{2,1,0:T(8,128)(2,1)S(1)}, bf16[3,16,512]{2,1,0:T(8,128)(2,1)S(1)}, u32[]{:S(2)}, u32[]{:S(2)}) collective-permute-start(bf16[3,16,512]{2,1,0:T(8,128)(2,1)S(1)} %pad_maximum_fusion.1.refs_0_), channel_id=1, source_target_pairs={{0,96},{16,112},{32,0},{48,16},{64,32},{80,48},{96,64},{112,80},{1... | collective-permute-start | bytes 147464 | tf_op jit(solution)/shard_map/ppermute | solution.py:72
  21.3 19.4 %collective-permute-start = (s16[2592,256]{1,0:T(8,128)(2,1)S(1)}, s16[2592,256]{1,0:T(8,128)(2,1)S(1)}, u32[]{:S(2)}, u32[]{:S(2)}) collective-permute-start(s16[2592,256]{1,0:T(8,128)(2,1)S(1)} %branch_0_fun.10), channel_id=1, source_target_pairs={{0,2},{1,3},{2,0},{3,1},{4,6},{5,7},{6,4},{7,5},{8,10},{9,11},{10,... | collective-permute-start | bytes 3981320 | tf_op jit(solution)/shard_map/cond/branch_0_fun/ppermute | solution.py:440
  33.1 22.2 %collective-permute-start.2 = (s16[2592,256]{1,0:T(8,128)(2,1)S(1)}, s16[2592,256]{1,0:T(8,128)(2,1)S(1)}, u32[]{:S(2)}, u32[]{:S(2)}) collective-permute-start(s16[2592,256]{1,0:T(8,128)(2,1)S(1)} %branch_0_fun.14), channel_id=1, source_target_pairs={{0,3},{1,0},{2,1},{3,2},{4,7},{5,4},{6,5},{7,6},{8,11},{9,8},{10,9... | collective-permute-start | bytes 3981320 | tf_op jit(solution)/shard_map/cond/branch_0_fun/ppermute | solution.py:440
  37.4 19.1 %collective-permute-start.1 = (s16[2592,256]{1,0:T(8,128)(2,1)S(1)}, s16[2592,256]{1,0:T(8,128)(2,1)S(1)}, u32[]{:S(2)}, u32[]{:S(2)}) collective-permute-start(s16[2592,256]{1,0:T(8,128)(2,1)S(1)} %branch_0_fun.13), channel_id=1, source_target_pairs={{0,1},{1,2},{2,3},{3,0},{4,5},{5,6},{6,7},{7,4},{8,9},{9,10},{10,1... | collective-permute-start | bytes 3981320 | tf_op jit(solution)/shard_map/cond/branch_0_fun/ppermute | solution.py:440
  57.2 9.2 %collective-permute-start.4 = (s16[672,256]{1,0:T(8,128)(2,1)S(1)}, s16[672,256]{1,0:T(8,128)(2,1)S(1)}, u32[]{:S(2)}, u32[]{:S(2)}) collective-permute-start(s16[672,256]{1,0:T(8,128)(2,1)S(1)} %branch_0_fun.16), channel_id=1, source_target_pairs={{0,8},{1,9},{2,10},{3,11},{4,12},{5,13},{6,14},{7,15},{8,0},{9,1},... | collective-permute-start | bytes 1032200 | tf_op jit(solution)/shard_map/cond/branch_0_fun/ppermute | solution.py:440
  63.1 8.5 %collective-permute-start.3 = (s16[672,256]{1,0:T(8,128)(2,1)S(1)}, s16[672,256]{1,0:T(8,128)(2,1)S(1)}, u32[]{:S(2)}, u32[]{:S(2)}) collective-permute-start(s16[672,256]{1,0:T(8,128)(2,1)S(1)} %get-tuple-element.57), channel_id=1, source_target_pairs={{0,4},{1,5},{2,6},{3,7},{4,8},{5,9},{6,10},{7,11},{8,12},{9,13},{1... | collective-permute-start | bytes 1032200 | tf_op jit(solution)/shard_map/cond/branch_0_fun/ppermute | solution.py:440
  64.2 7.4 %collective-permute-start.5 = (s16[672,256]{1,0:T(8,128)(2,1)S(1)}, s16[672,256]{1,0:T(8,128)(2,1)S(1)}, u32[]{:S(2)}, u32[]{:S(2)}) collective-permute-start(s16[672,256]{1,0:T(8,128)(2,1)S(1)} %get-tuple-element.58), channel_id=1, source_target_pairs={{0,12},{1,13},{2,14},{3,15},{4,0},{5,1},{6,2},{7,3},{8,4},{9,5},{1... | collective-permute-start | bytes 1032200 | tf_op jit(solution)/shard_map/cond/branch_0_fun/ppermute | solution.py:440
  72.0 8.4 %collective-permute-start.6 = (bf16[640,256]{1,0:T(8,128)(2,1)S(1)}, bf16[640,256]{1,0:T(8,128)(2,1)S(1)}, u32[]{:S(2)}, u32[]{:S(2)}) collective-permute-start(bf16[640,256]{1,0:T(8,128)(2,1)S(1)} %branch_0_fun.17.r0), channel_id=1, source_target_pairs={{0,4},{1,5},{2,6},{3,7},{4,8},{5,9},{6,10},{7,11},{8,12},{9,13},{1... | collective-permute-start | bytes 983048 | tf_op jit(solution)/shard_map/cond/branch_0_fun/ppermute | solution.py:440
  72.6 12.8 %collective-permute-start.7 = (bf16[640,256]{1,0:T(8,128)(2,1)S(1)}, bf16[640,256]{1,0:T(8,128)(2,1)S(1)}, u32[]{:S(2)}, u32[]{:S(2)}) collective-permute-start(bf16[640,256]{1,0:T(8,128)(2,1)S(1)} %branch_0_fun.17.r0), channel_id=1, source_target_pairs={{0,8},{1,9},{2,10},{3,11},{4,12},{5,13},{6,14},{7,15},{8,0},{9,1},... | collective-permute-start | bytes 983048 | tf_op jit(solution)/shard_map/cond/branch_0_fun/ppermute | solution.py:440
  76.8 9.0 %collective-permute-start.8 = (bf16[640,256]{1,0:T(8,128)(2,1)S(1)}, bf16[640,256]{1,0:T(8,128)(2,1)S(1)}, u32[]{:S(2)}, u32[]{:S(2)}) collective-permute-start(bf16[640,256]{1,0:T(8,128)(2,1)S(1)} %branch_0_fun.17.r0), channel_id=1, source_target_pairs={{0,12},{1,13},{2,14},{3,15},{4,0},{5,1},{6,2},{7,3},{8,4},{9,5},{1... | collective-permute-start | bytes 983048 | tf_op jit(solution)/shard_map/cond/branch_0_fun/ppermute | solution.py:440
  85.9 24.1 %collective-permute-start.10 = (bf16[2560,256]{1,0:T(8,128)(2,1)S(1)}, bf16[2560,256]{1,0:T(8,128)(2,1)S(1)}, u32[]{:S(2)}, u32[]{:S(2)}) collective-permute-start(bf16[2560,256]{1,0:T(8,128)(2,1)S(1)} %bitcast.26), channel_id=1, source_target_pairs={{0,3},{1,0},{2,1},{3,2},{4,7},{5,4},{6,5},{7,6},{8,11},{9,8},{10,9... | collective-permute-start | bytes 3932168 | tf_op jit(solution)/shard_map/cond/branch_0_fun/ppermute | solution.py:440
  87.0 23.0 %collective-permute-start.11 = (bf16[2560,256]{1,0:T(8,128)(2,1)S(1)}, bf16[2560,256]{1,0:T(8,128)(2,1)S(1)}, u32[]{:S(2)}, u32[]{:S(2)}) collective-permute-start(bf16[2560,256]{1,0:T(8,128)(2,1)S(1)} %bitcast.27), channel_id=1, source_target_pairs={{0,2},{1,3},{2,0},{3,1},{4,6},{5,7},{6,4},{7,5},{8,10},{9,11},{10,... | collective-permute-start | bytes 3932168 | tf_op jit(solution)/shard_map/cond/branch_0_fun/ppermute | solution.py:440
  87.8 32.4 %collective-permute-start.9 = (bf16[2560,256]{1,0:T(8,128)(2,1)S(1)}, bf16[2560,256]{1,0:T(8,128)(2,1)S(1)}, u32[]{:S(2)}, u32[]{:S(2)}) collective-permute-start(bf16[2560,256]{1,0:T(8,128)(2,1)S(1)} %bitcast.28), channel_id=1, source_target_pairs={{0,1},{1,2},{2,3},{3,0},{4,5},{5,6},{6,7},{7,4},{8,9},{9,10},{10,1... | collective-permute-start | bytes 3932168 | tf_op jit(solution)/shard_map/cond/branch_0_fun/ppermute | solution.py:440
  88.6 6.3 %collective-permute-start.13 = (f32[64,512]{1,0:T(8,128)S(1)}, f32[64,512]{1,0:T(8,128)S(1)}, u32[]{:S(2)}, u32[]{:S(2)}) collective-permute-start(f32[64,512]{1,0:T(8,128)S(1)} %get-tuple-element.59.refs_6_), channel_id=1, source_target_pairs={{0,32},{16,48},{32,64},{48,80},{64,96},{80,112},{96,0},{112,16},{1... | collective-permute-start | bytes 393224 | tf_op jit(solution)/shard_map/cond/branch_0_fun/ppermute | solution.py:72
  93.9 5.9 %collective-permute-start.14 = (f32[64,512]{1,0:T(8,128)S(1)}, f32[64,512]{1,0:T(8,128)S(1)}, u32[]{:S(2)}, u32[]{:S(2)}) collective-permute-start(f32[64,512]{1,0:T(8,128)S(1)} %get-tuple-element.59.refs_6_), channel_id=1, source_target_pairs={{0,48},{16,64},{32,80},{48,96},{64,112},{80,0},{96,16},{112,32},{1... | collective-permute-start | bytes 393224 | tf_op jit(solution)/shard_map/cond/branch_0_fun/ppermute | solution.py:72
  95.0 7.5 %collective-permute-start.15 = (f32[64,512]{1,0:T(8,128)S(1)}, f32[64,512]{1,0:T(8,128)S(1)}, u32[]{:S(2)}, u32[]{:S(2)}) collective-permute-start(f32[64,512]{1,0:T(8,128)S(1)} %get-tuple-element.59.refs_6_), channel_id=1, source_target_pairs={{0,64},{16,80},{32,96},{48,112},{64,0},{80,16},{96,32},{112,48},{1... | collective-permute-start | bytes 393224 | tf_op jit(solution)/shard_map/cond/branch_0_fun/ppermute | solution.py:72
  99.8 5.9 %collective-permute-start.16 = (f32[64,512]{1,0:T(8,128)S(1)}, f32[64,512]{1,0:T(8,128)S(1)}, u32[]{:S(2)}, u32[]{:S(2)}) collective-permute-start(f32[64,512]{1,0:T(8,128)S(1)} %get-tuple-element.59.refs_6_), channel_id=1, source_target_pairs={{0,80},{16,96},{32,112},{48,0},{64,16},{80,32},{96,48},{112,64},{1... | collective-permute-start | bytes 393224 | tf_op jit(solution)/shard_map/cond/branch_0_fun/ppermute | solution.py:72
  102.4 7.6 %collective-permute-start.17 = (f32[64,512]{1,0:T(8,128)S(1)}, f32[64,512]{1,0:T(8,128)S(1)}, u32[]{:S(2)}, u32[]{:S(2)}) collective-permute-start(f32[64,512]{1,0:T(8,128)S(1)} %get-tuple-element.59.refs_6_), channel_id=1, source_target_pairs={{0,96},{16,112},{32,0},{48,16},{64,32},{80,48},{96,64},{112,80},{1... | collective-permute-start | bytes 393224 | tf_op jit(solution)/shard_map/cond/branch_0_fun/ppermute | solution.py:72
  147.6 11.1 %all-to-all-start.1 = ((f32[16,6,128]{2,1,0:T(8,128)}), f32[16,6,128]{2,1,0:T(8,128)S(1)}, u32[]{:S(2)}, u32[]{:S(2)}) async-start(f32[16,6,128]{2,1,0:T(8,128)} %broadcast_in_dim_broadcast_in_dim_broadcast_in_dim.2), calls=%async_computation.1 | async-start | bytes 131072 | tf_op jit(solution)/shard_map/all_to_all | solution.py:468
  (9 other events, 225.4 us)
where the time goes:
time: 160 us
  waiting for transfers between devices  70.9 us (44%)
  Pallas kernels  36.1 us (23%)
  starting transfers between devices  32.3 us (20%)
  blocking collectives  11.9 us (7%)
  other arithmetic  5.11 us (3%)
  local copies, waits for them, and re-layouts  1.76 us (1%)
    ppermute x12, waiting for transfers between devices, send(): lax.ppermute(x, ('core', 'z', 'y'), shifts(first, s))  39.5 us
    ppermute x14, waiting for transfers between devices, ring_of(): lax.ppermute(x, ('x', 'core'), [(i, (i + s) % n) for i in range(n)])  23.9 us
    ppermute x12, starting transfers between devices, send(): lax.ppermute(x, ('core', 'z', 'y'), shifts(first, s))  20.1 us
    pallas_call x1, Pallas kernels, final_grads(): pl.pallas_call(functools.partial(final_kernel, which, nblk), out_shape=ja...  12.2 us
    all_to_all x1, blocking collectives, body(): raw = jnp.sum(lax.all_to_all(owned, param, 0, 0, tiled=True), axis=0)  11.9 us
    pallas_call x3, Pallas kernels, partial_piece(): pl.pallas_call(functools.partial(partial_kernel, nblk, s), out_shape=jax....  9.18 us
    ppermute x14, starting transfers between devices, ring_of(): lax.ppermute(x, ('x', 'core'), [(i, (i + s) % n) for i in range(n)])  8.69 us
    all_to_all x1, waiting for transfers between devices, share(): lax.all_to_all(jnp.broadcast_to(x[None], (n,) + x.shape), axes, 0, 0, til...  7.53 us
  transfers between devices with their start and end apart: 27, of which 18 were waited for; matrix products, arithmetic and copies ran while one was open for 1% of the time, Pallas kernels for 10%

commit v1 on v0

--- a/solution.py
+++ b/solution.py
@@ -387,10 +387,8 @@
             )
             big, rest = two_parts(pre)
             both = lax.dot_general(big, wide2[i], nt, preferred_element_type=F32)
-            wide = both[:, :64] + (
-                both[:, 64:]
-                + lax.dot_general(rest, wide2[i, :64, :], nt, preferred_element_type=F32)
-            )
+            small = lax.dot_general(rest, wide2[i], nt, preferred_element_type=F32)
+            wide = both[:, :64] + (both[:, 64:] + (small[:, :64] + small[:, 64:]))
             for k in range(2):
                 out[2 * j + k, i * 64 : (i + 1) * 64, :] = jnp.dot(
                     sides[i],

time: 160 us -> 160 us (level)
  no operation moved by 1% of the time
where the time goes in v1:
time: 160 us; the launch traced here: 159 us
  waiting for transfers between devices  71.1 us (44%)
  Pallas kernels  35.5 us (22%)
  starting transfers between devices  32.2 us (20%)
  blocking collectives  11.9 us (7%)
  other arithmetic  5.11 us (3%)
  local copies, waits for them, and re-layouts  1.76 us (1%)
    ppermute x12, waiting for transfers between devices, send(): lax.ppermute(x, ('core', 'z', 'y'), shifts(first, s))  39.6 us
    ppermute x14, waiting for transfers between devices, ring_of(): lax.ppermute(x, ('x', 'core'), [(i, (i + s) % n) for i in range(n)])  23.9 us
    ppermute x12, starting transfers between devices, send(): lax.ppermute(x, ('core', 'z', 'y'), shifts(first, s))  20 us
    all_to_all x1, blocking collectives, body(): raw = jnp.sum(lax.all_to_all(owned, param, 0, 0, tiled=True), axis=0)  11.9 us
    pallas_call x1, Pallas kernels, final_grads(): pl.pallas_call(functools.partial(final_kernel, which, nblk), out_shape=ja...  11.6 us
    pallas_call x3, Pallas kernels, partial_piece(): pl.pallas_call(functools.partial(partial_kernel, nblk, s), out_shape=jax....  9.18 us
    ppermute x14, starting transfers between devices, ring_of(): lax.ppermute(x, ('x', 'core'), [(i, (i + s) % n) for i in range(n)])  8.62 us
    all_to_all x1, waiting for transfers between devices, share(): lax.all_to_all(jnp.broadcast_to(x[None], (n,) + x.shape), axes, 0, 0, til...  7.53 us
  transfers between devices with their start and end apart: 27, of which 18 were waited for; matrix products, arithmetic and copies ran while one was open for 1% of the time, Pallas kernels for 10%

profile of v1, /device:TPU:6, one launch (start us, length us, event | category | flops | bytes accessed | tf_op | source)
XLA Modules:
  0.0 159.0 jit_solution(8186433444659841045)
XLA Ops:
  1.9 2.4 %collective-permute-start.40 = (bf16[3,16,512]{2,1,0:T(8,128)(2,1)S(1)}, bf16[3,16,512]{2,1,0:T(8,128)(2,1)S(1)}, u32[]{:S(2)}, u32[]{:S(2)}) collective-permute-start(bf16[3,16,512]{2,1,0:T(8,128)(2,1)S(1)} %pad_maximum_fusion.1.refs_0_), channel_id=1, source_target_pairs={{0,48},{16,64},{32,80},{48,96},{64,112},{80,0},{96,16},{112,32},{1... | collective-permute-start | bytes 147464 | tf_op jit(solution)/shard_map/ppermute | solution.py:72
  11.0 2.6 %collective-permute-done.43.refs_6_ = bf16[3,16,512]{2,1,0:T(8,128)(2,1)S(1)} collective-permute-done((bf16[3,16,512]{2,1,0:T(8,128)(2,1)S(1)}, bf16[3,16,512]{2,1,0:T(8,128)(2,1)S(1)}, u32[]{:S(2)}, u32[]{:S(2)}) %collective-permute-start.43) | collective-permute-done | bytes 49184 | tf_op jit(solution)/shard_map/ppermute | solution.py:72
  15.2 117.0 %conditional.1 = (f32[6,128,64]{2,1,0:T(8,128)S(1)}) conditional(s32[]{:T(128)} %clamp.3, (s32[6]{0:T(128)}, bf16[2,512,128]{2,1,0:T(8,128)(2,1)S(1)}, bf16[6,2048,512]{2,1,0:T(8,128)(2,1)}, bf16[6,2048,512]{2,1,0:T(8,128)(2,1)}, f32[64,512]{1,0:T(8,128)S(1)}, /*index=5*/f32[64,128]{1,0:T(8,128)}, f32[64,512]{1,0:T(8,128)}, f32[64,512]{1,0:T(8,128)}, ...), branch_computations={%region_2.3_spmd, %region_3.4_spmd} | conditional | flops 3229093888 | bytes 240128960 | solution.py:491
  15.2 6.1 %branch_0_fun.10 = s16[2592,256]{1,0:T(8,128)(2,1)S(1)} custom-call(s32[6]{0:T(128)} %get-tuple-element.48.lens, bf16[2,512,128]{2,1,0:T(8,128)(2,1)S(1)} %get-tuple-element.45.w, bf16[6,2048,512]{2,1,0:T(8,128)(2,1)} %get-tuple-element.49.a_hbm, bf16[6,2048,512]{2,1,0:T(8,128)(2,1)} %get-tuple-element.50.g_hbm), custom_call_target="tpu_custom_call" | custom-call | flops 1000 | bytes 1000 | tf_op jit(solution)/shard_map/cond/branch_0_fun/pallas_call | solution.py:206
  21.3 3.3 %collective-permute-start = (s16[2592,256]{1,0:T(8,128)(2,1)S(1)}, s16[2592,256]{1,0:T(8,128)(2,1)S(1)}, u32[]{:S(2)}, u32[]{:S(2)}) collective-permute-start(s16[2592,256]{1,0:T(8,128)(2,1)S(1)} %branch_0_fun.10), channel_id=1, source_target_pairs={{0,2},{1,3},{2,0},{3,1},{4,6},{5,7},{6,4},{7,5},{8,10},{9,11},{10,... | collective-permute-start | bytes 3981320 | tf_op jit(solution)/shard_map/cond/branch_0_fun/ppermute | solution.py:438
  24.6 5.4 %branch_0_fun.11 = (bf16[6,2048,512]{2,1,0:T(8,128)(2,1)S(1)}, bf16[6,2048,512]{2,1,0:T(8,128)(2,1)S(1)}) custom-call(bf16[6,2048,512]{2,1,0:T(8,128)(2,1)S(1)} %copy-done.2, bf16[6,2048,512]{2,1,0:T(8,128)(2,1)} %get-tuple-element.50.g_hbm), custom_call_target="tpu_custom_call" | custom-call | bytes 25165824 | tf_op jit(solution)/shard_map/cond/branch_0_fun/pallas_call | solution.py:89
  30.0 3.1 %branch_0_fun.14 = s16[2592,256]{1,0:T(8,128)(2,1)S(1)} custom-call(s32[6]{0:T(128)S(1)} %copy-done.12, bf16[2,512,128]{2,1,0:T(8,128)(2,1)S(1)} %get-tuple-element.45.w, bf16[6,2048,512]{2,1,0:T(8,128)(2,1)S(1)} %get-tuple-element.51.a.refs_4_, bf16[6,2048,512]{2,1,0:T(8,128)(2,1)S(1)} %get-tuple-element.52.g.refs_5_), custom_call_target="tpu_custom_call" | custom-call | flops 1000 | bytes 1000 | tf_op jit(solution)/shard_map/cond/branch_0_fun/pallas_call | solution.py:152
  34.4 3.1 %branch_0_fun.13 = s16[2592,256]{1,0:T(8,128)(2,1)S(1)} custom-call(s32[6]{0:T(128)S(1)} %copy-done.12, bf16[2,512,128]{2,1,0:T(8,128)(2,1)S(1)} %get-tuple-element.45.w, bf16[6,2048,512]{2,1,0:T(8,128)(2,1)S(1)} %get-tuple-element.51.a.refs_4_, bf16[6,2048,512]{2,1,0:T(8,128)(2,1)S(1)} %get-tuple-element.52.g.refs_5_), custom_call_target="tpu_custom_call" | custom-call | flops 1000 | bytes 1000 | tf_op jit(solution)/shard_map/cond/branch_0_fun/pallas_call | solution.py:152
  40.7 3.1 %branch_0_fun.12.q0 = s16[2592,256]{1,0:T(8,128)(2,1)S(1)} custom-call(s32[6]{0:T(128)S(1)} %copy-done.12, bf16[2,512,128]{2,1,0:T(8,128)(2,1)S(1)} %get-tuple-element.45.w, bf16[6,2048,512]{2,1,0:T(8,128)(2,1)S(1)} %get-tuple-element.51.a.refs_4_, bf16[6,2048,512]{2,1,0:T(8,128)(2,1)S(1)} %get-tuple-element.52.g.refs_5_), custom_call_target="tpu_custom_call" | custom-call | flops 1000 | bytes 1000 | tf_op jit(solution)/shard_map/cond/branch_0_fun/pallas_call | solution.py:152
  43.7 11.5 %collective-permute-done.2.q3 = s16[2592,256]{1,0:T(8,128)(2,1)S(1)} collective-permute-done((s16[2592,256]{1,0:T(8,128)(2,1)S(1)}, s16[2592,256]{1,0:T(8,128)(2,1)S(1)}, u32[]{:S(2)}, u32[]{:S(2)}) %collective-permute-start.2) | collective-permute-done | bytes 1327136 | tf_op jit(solution)/shard_map/cond/branch_0_fun/ppermute | solution.py:438
  57.2 4.0 %collective-permute-start.4 = (s16[672,256]{1,0:T(8,128)(2,1)S(1)}, s16[672,256]{1,0:T(8,128)(2,1)S(1)}, u32[]{:S(2)}, u32[]{:S(2)}) collective-permute-start(s16[672,256]{1,0:T(8,128)(2,1)S(1)} %branch_0_fun.16), channel_id=1, source_target_pairs={{0,8},{1,9},{2,10},{3,11},{4,12},{5,13},{6,14},{7,15},{8,0},{9,1},... | collective-permute-start | bytes 1032200 | tf_op jit(solution)/shard_map/cond/branch_0_fun/ppermute | solution.py:438
  66.5 5.2 %collective-permute-done.3.r1 = s16[672,256]{1,0:T(8,128)(2,1)S(1)} collective-permute-done((s16[672,256]{1,0:T(8,128)(2,1)S(1)}, s16[672,256]{1,0:T(8,128)(2,1)S(1)}, u32[]{:S(2)}, u32[]{:S(2)}) %collective-permute-start.3) | collective-permute-done | bytes 344096 | tf_op jit(solution)/shard_map/cond/branch_0_fun/ppermute | solution.py:438
  72.7 4.2 %collective-permute-start.7 = (bf16[640,256]{1,0:T(8,128)(2,1)S(1)}, bf16[640,256]{1,0:T(8,128)(2,1)S(1)}, u32[]{:S(2)}, u32[]{:S(2)}) collective-permute-start(bf16[640,256]{1,0:T(8,128)(2,1)S(1)} %branch_0_fun.17.r0), channel_id=1, source_target_pairs={{0,8},{1,9},{2,10},{3,11},{4,12},{5,13},{6,14},{7,15},{8,0},{9,1},... | collective-permute-start | bytes 983048 | tf_op jit(solution)/shard_map/cond/branch_0_fun/ppermute | solution.py:438
  76.9 3.6 %collective-permute-done.6.r1 = bf16[640,256]{1,0:T(8,128)(2,1)S(1)} collective-permute-done((bf16[640,256]{1,0:T(8,128)(2,1)S(1)}, bf16[640,256]{1,0:T(8,128)(2,1)S(1)}, u32[]{:S(2)}, u32[]{:S(2)}) %collective-permute-start.6) | collective-permute-done | bytes 327712 | tf_op jit(solution)/shard_map/cond/branch_0_fun/ppermute | solution.py:438
  80.5 5.0 %collective-permute-done.7.r2 = bf16[640,256]{1,0:T(8,128)(2,1)S(1)} collective-permute-done((bf16[640,256]{1,0:T(8,128)(2,1)S(1)}, bf16[640,256]{1,0:T(8,128)(2,1)S(1)}, u32[]{:S(2)}, u32[]{:S(2)}) %collective-permute-start.7) | collective-permute-done | bytes 327712 | tf_op jit(solution)/shard_map/cond/branch_0_fun/ppermute | solution.py:438
  89.2 4.6 %collective-permute-done.12.refs_7_ = f32[64,512]{1,0:T(8,128)S(1)} collective-permute-done((f32[64,512]{1,0:T(8,128)S(1)}, f32[64,512]{1,0:T(8,128)S(1)}, u32[]{:S(2)}, u32[]{:S(2)}) %collective-permute-start.12) | collective-permute-done | bytes 131104 | tf_op jit(solution)/shard_map/cond/branch_0_fun/ppermute | solution.py:72
  95.4 4.4 %collective-permute-done.14.refs_9_ = f32[64,512]{1,0:T(8,128)S(1)} collective-permute-done((f32[64,512]{1,0:T(8,128)S(1)}, f32[64,512]{1,0:T(8,128)S(1)}, u32[]{:S(2)}, u32[]{:S(2)}) %collective-permute-start.14) | collective-permute-done | bytes 131104 | tf_op jit(solution)/shard_map/cond/branch_0_fun/ppermute | solution.py:72
  102.4 3.3 %collective-permute-done.16.refs_11_ = f32[64,512]{1,0:T(8,128)S(1)} collective-permute-done((f32[64,512]{1,0:T(8,128)S(1)}, f32[64,512]{1,0:T(8,128)S(1)}, u32[]{:S(2)}, u32[]{:S(2)}) %collective-permute-start.16) | collective-permute-done | bytes 131104 | tf_op jit(solution)/shard_map/cond/branch_0_fun/ppermute | solution.py:72
  105.7 4.3 %collective-permute-done.17.refs_12_ = f32[64,512]{1,0:T(8,128)S(1)} collective-permute-done((f32[64,512]{1,0:T(8,128)S(1)}, f32[64,512]{1,0:T(8,128)S(1)}, u32[]{:S(2)}, u32[]{:S(2)}) %collective-permute-start.17) | collective-permute-done | bytes 131104 | tf_op jit(solution)/shard_map/cond/branch_0_fun/ppermute | solution.py:72
  110.0 10.2 %collective-permute-done.9.refs_1_ = bf16[2560,256]{1,0:T(8,128)(2,1)S(1)} collective-permute-done((bf16[2560,256]{1,0:T(8,128)(2,1)S(1)}, bf16[2560,256]{1,0:T(8,128)(2,1)S(1)}, u32[]{:S(2)}, u32[]{:S(2)}) %collective-permute-start.9) | collective-permute-done | bytes 1310752 | tf_op jit(solution)/shard_map/cond/branch_0_fun/ppermute | solution.py:438
  120.1 11.6 %branch_0_fun.19 = f32[6,128,64]{2,1,0:T(8,128)S(1)} custom-call(s32[6]{0:T(128)S(1)} %copy-done.12, bf16[2560,256]{1,0:T(8,128)(2,1)S(1)} %bitcast.29, bf16[2560,256]{1,0:T(8,128)(2,1)S(1)} %collective-permute-done.9.refs_1_, bf16[2560,256]{1,0:T(8,128)(2,1)S(1)} %collective-permute-done.10.refs_2_, bf16[2560,256]{1,0:T(8,128)(2,1)S(1)} %collective-permute-done.11.refs_3_, ...), custom_call_target="tpu_custom_call" | custom-call | flops 2684354560 | bytes 5242880 | tf_op jit(solution)/shard_map/cond/branch_0_fun/pallas_call | solution.py:405
  132.5 11.9 %all_to_all.10 = f32[16,1,3072]{2,1,0:T(1,128)S(1)} all-to-all(f32[16,1,3072]{2,1,0:T(1,128)S(1)} %reshape.31), channel_id=1, replica_groups=mesh['x'=4,'core'=2,'z'=4,'y'=4] {'z','y'}, dimensions={0} | all-to-all | bytes 393216 | tf_op jit(solution)/shard_map/all_to_all | solution.py:502
  147.1 3.5 %all-to-all-start.1 = ((f32[16,6,128]{2,1,0:T(8,128)}), f32[16,6,128]{2,1,0:T(8,128)S(1)}, u32[]{:S(2)}, u32[]{:S(2)}) async-start(f32[16,6,128]{2,1,0:T(8,128)} %broadcast_in_dim_broadcast_in_dim_broadcast_in_dim.2), calls=%async_computation.1 | async-start | bytes 131072 | tf_op jit(solution)/shard_map/all_to_all | solution.py:466
  150.7 7.5 %all-to-all-done.1 = f32[16,6,128]{2,1,0:T(8,128)S(1)} async-done(((f32[16,6,128]{2,1,0:T(8,128)}), f32[16,6,128]{2,1,0:T(8,128)S(1)}, u32[]{:S(2)}, u32[]{:S(2)}) %all-to-all-start.1) | async-done | bytes 49184 | tf_op jit(solution)/shard_map/all_to_all | solution.py:466
  (83 shorter events, 33.9 us)
Async XLA Ops:
  1.4 6.8 %collective-permute-start.38 = (bf16[3,16,512]{2,1,0:T(8,128)(2,1)S(1)}, bf16[3,16,512]{2,1,0:T(8,128)(2,1)S(1)}, u32[]{:S(2)}, u32[]{:S(2)}) collective-permute-start(bf16[3,16,512]{2,1,0:T(8,128)(2,1)S(1)} %pad_maximum_fusion.1.refs_0_), channel_id=1, source_target_pairs={{0,16},{16,32},{32,48},{48,64},{64,80},{80,96},{96,112},{112,0},{1... | collective-permute-start | bytes 147464 | tf_op jit(solution)/shard_map/ppermute | solution.py:72
  1.4 6.9 %collective-permute-start.39 = (bf16[3,16,512]{2,1,0:T(8,128)(2,1)S(1)}, bf16[3,16,512]{2,1,0:T(8,128)(2,1)S(1)}, u32[]{:S(2)}, u32[]{:S(2)}) collective-permute-start(bf16[3,16,512]{2,1,0:T(8,128)(2,1)S(1)} %pad_maximum_fusion.1.refs_0_), channel_id=1, source_target_pairs={{0,32},{16,48},{32,64},{48,80},{64,96},{80,112},{96,0},{112,16},{1... | collective-permute-start | bytes 147464 | tf_op jit(solution)/shard_map/ppermute | solution.py:72
  1.9 7.4 %collective-permute-start.40 = (bf16[3,16,512]{2,1,0:T(8,128)(2,1)S(1)}, bf16[3,16,512]{2,1,0:T(8,128)(2,1)S(1)}, u32[]{:S(2)}, u32[]{:S(2)}) collective-permute-start(bf16[3,16,512]{2,1,0:T(8,128)(2,1)S(1)} %pad_maximum_fusion.1.refs_0_), channel_id=1, source_target_pairs={{0,48},{16,64},{32,80},{48,96},{64,112},{80,0},{96,16},{112,32},{1... | collective-permute-start | bytes 147464 | tf_op jit(solution)/shard_map/ppermute | solution.py:72
  4.3 5.6 %collective-permute-start.41 = (bf16[3,16,512]{2,1,0:T(8,128)(2,1)S(1)}, bf16[3,16,512]{2,1,0:T(8,128)(2,1)S(1)}, u32[]{:S(2)}, u32[]{:S(2)}) collective-permute-start(bf16[3,16,512]{2,1,0:T(8,128)(2,1)S(1)} %pad_maximum_fusion.1.refs_0_), channel_id=1, source_target_pairs={{0,64},{16,80},{32,96},{48,112},{64,0},{80,16},{96,32},{112,48},{1... | collective-permute-start | bytes 147464 | tf_op jit(solution)/shard_map/ppermute | solution.py:72
  5.4 5.6 %collective-permute-start.42 = (bf16[3,16,512]{2,1,0:T(8,128)(2,1)S(1)}, bf16[3,16,512]{2,1,0:T(8,128)(2,1)S(1)}, u32[]{:S(2)}, u32[]{:S(2)}) collective-permute-start(bf16[3,16,512]{2,1,0:T(8,128)(2,1)S(1)} %pad_maximum_fusion.1.refs_0_), channel_id=1, source_target_pairs={{0,80},{16,96},{32,112},{48,0},{64,16},{80,32},{96,48},{112,64},{1... | collective-permute-start | bytes 147464 | tf_op jit(solution)/shard_map/ppermute | solution.py:72
  8.2 5.4 %collective-permute-start.43 = (bf16[3,16,512]{2,1,0:T(8,128)(2,1)S(1)}, bf16[3,16,512]{2,1,0:T(8,128)(2,1)S(1)}, u32[]{:S(2)}, u32[]{:S(2)}) collective-permute-start(bf16[3,16,512]{2,1,0:T(8,128)(2,1)S(1)} %pad_maximum_fusion.1.refs_0_), channel_id=1, source_target_pairs={{0,96},{16,112},{32,0},{48,16},{64,32},{80,48},{96,64},{112,80},{1... | collective-permute-start | bytes 147464 | tf_op jit(solution)/shard_map/ppermute | solution.py:72
  21.3 19.4 %collective-permute-start = (s16[2592,256]{1,0:T(8,128)(2,1)S(1)}, s16[2592,256]{1,0:T(8,128)(2,1)S(1)}, u32[]{:S(2)}, u32[]{:S(2)}) collective-permute-start(s16[2592,256]{1,0:T(8,128)(2,1)S(1)} %branch_0_fun.10), channel_id=1, source_target_pairs={{0,2},{1,3},{2,0},{3,1},{4,6},{5,7},{6,4},{7,5},{8,10},{9,11},{10,... | collective-permute-start | bytes 3981320 | tf_op jit(solution)/shard_map/cond/branch_0_fun/ppermute | solution.py:438
  33.1 22.2 %collective-permute-start.2 = (s16[2592,256]{1,0:T(8,128)(2,1)S(1)}, s16[2592,256]{1,0:T(8,128)(2,1)S(1)}, u32[]{:S(2)}, u32[]{:S(2)}) collective-permute-start(s16[2592,256]{1,0:T(8,128)(2,1)S(1)} %branch_0_fun.14), channel_id=1, source_target_pairs={{0,3},{1,0},{2,1},{3,2},{4,7},{5,4},{6,5},{7,6},{8,11},{9,8},{10,9... | collective-permute-start | bytes 3981320 | tf_op jit(solution)/shard_map/cond/branch_0_fun/ppermute | solution.py:438
  37.5 19.1 %collective-permute-start.1 = (s16[2592,256]{1,0:T(8,128)(2,1)S(1)}, s16[2592,256]{1,0:T(8,128)(2,1)S(1)}, u32[]{:S(2)}, u32[]{:S(2)}) collective-permute-start(s16[2592,256]{1,0:T(8,128)(2,1)S(1)} %branch_0_fun.13), channel_id=1, source_target_pairs={{0,1},{1,2},{2,3},{3,0},{4,5},{5,6},{6,7},{7,4},{8,9},{9,10},{10,1... | collective-permute-start | bytes 3981320 | tf_op jit(solution)/shard_map/cond/branch_0_fun/ppermute | solution.py:438
  57.2 9.2 %collective-permute-start.4 = (s16[672,256]{1,0:T(8,128)(2,1)S(1)}, s16[672,256]{1,0:T(8,128)(2,1)S(1)}, u32[]{:S(2)}, u32[]{:S(2)}) collective-permute-start(s16[672,256]{1,0:T(8,128)(2,1)S(1)} %branch_0_fun.16), channel_id=1, source_target_pairs={{0,8},{1,9},{2,10},{3,11},{4,12},{5,13},{6,14},{7,15},{8,0},{9,1},... | collective-permute-start | bytes 1032200 | tf_op jit(solution)/shard_map/cond/branch_0_fun/ppermute | solution.py:438
  63.1 8.5 %collective-permute-start.3 = (s16[672,256]{1,0:T(8,128)(2,1)S(1)}, s16[672,256]{1,0:T(8,128)(2,1)S(1)}, u32[]{:S(2)}, u32[]{:S(2)}) collective-permute-start(s16[672,256]{1,0:T(8,128)(2,1)S(1)} %get-tuple-element.57), channel_id=1, source_target_pairs={{0,4},{1,5},{2,6},{3,7},{4,8},{5,9},{6,10},{7,11},{8,12},{9,13},{1... | collective-permute-start | bytes 1032200 | tf_op jit(solution)/shard_map/cond/branch_0_fun/ppermute | solution.py:438
  64.2 7.4 %collective-permute-start.5 = (s16[672,256]{1,0:T(8,128)(2,1)S(1)}, s16[672,256]{1,0:T(8,128)(2,1)S(1)}, u32[]{:S(2)}, u32[]{:S(2)}) collective-permute-start(s16[672,256]{1,0:T(8,128)(2,1)S(1)} %get-tuple-element.58), channel_id=1, source_target_pairs={{0,12},{1,13},{2,14},{3,15},{4,0},{5,1},{6,2},{7,3},{8,4},{9,5},{1... | collective-permute-start | bytes 1032200 | tf_op jit(solution)/shard_map/cond/branch_0_fun/ppermute | solution.py:438
  72.1 8.4 %collective-permute-start.6 = (bf16[640,256]{1,0:T(8,128)(2,1)S(1)}, bf16[640,256]{1,0:T(8,128)(2,1)S(1)}, u32[]{:S(2)}, u32[]{:S(2)}) collective-permute-start(bf16[640,256]{1,0:T(8,128)(2,1)S(1)} %branch_0_fun.17.r0), channel_id=1, source_target_pairs={{0,4},{1,5},{2,6},{3,7},{4,8},{5,9},{6,10},{7,11},{8,12},{9,13},{1... | collective-permute-start | bytes 983048 | tf_op jit(solution)/shard_map/cond/branch_0_fun/ppermute | solution.py:438
  72.7 12.8 %collective-permute-start.7 = (bf16[640,256]{1,0:T(8,128)(2,1)S(1)}, bf16[640,256]{1,0:T(8,128)(2,1)S(1)}, u32[]{:S(2)}, u32[]{:S(2)}) collective-permute-start(bf16[640,256]{1,0:T(8,128)(2,1)S(1)} %branch_0_fun.17.r0), channel_id=1, source_target_pairs={{0,8},{1,9},{2,10},{3,11},{4,12},{5,13},{6,14},{7,15},{8,0},{9,1},... | collective-permute-start | bytes 983048 | tf_op jit(solution)/shard_map/cond/branch_0_fun/ppermute | solution.py:438
  76.9 9.1 %collective-permute-start.8 = (bf16[640,256]{1,0:T(8,128)(2,1)S(1)}, bf16[640,256]{1,0:T(8,128)(2,1)S(1)}, u32[]{:S(2)}, u32[]{:S(2)}) collective-permute-start(bf16[640,256]{1,0:T(8,128)(2,1)S(1)} %branch_0_fun.17.r0), channel_id=1, source_target_pairs={{0,12},{1,13},{2,14},{3,15},{4,0},{5,1},{6,2},{7,3},{8,4},{9,5},{1... | collective-permute-start | bytes 983048 | tf_op jit(solution)/shard_map/cond/branch_0_fun/ppermute | solution.py:438
  86.1 23.9 %collective-permute-start.10 = (bf16[2560,256]{1,0:T(8,128)(2,1)S(1)}, bf16[2560,256]{1,0:T(8,128)(2,1)S(1)}, u32[]{:S(2)}, u32[]{:S(2)}) collective-permute-start(bf16[2560,256]{1,0:T(8,128)(2,1)S(1)} %bitcast.26), channel_id=1, source_target_pairs={{0,3},{1,0},{2,1},{3,2},{4,7},{5,4},{6,5},{7,6},{8,11},{9,8},{10,9... | collective-permute-start | bytes 3932168 | tf_op jit(solution)/shard_map/cond/branch_0_fun/ppermute | solution.py:438
  87.0 23.0 %collective-permute-start.11 = (bf16[2560,256]{1,0:T(8,128)(2,1)S(1)}, bf16[2560,256]{1,0:T(8,128)(2,1)S(1)}, u32[]{:S(2)}, u32[]{:S(2)}) collective-permute-start(bf16[2560,256]{1,0:T(8,128)(2,1)S(1)} %bitcast.27), channel_id=1, source_target_pairs={{0,2},{1,3},{2,0},{3,1},{4,6},{5,7},{6,4},{7,5},{8,10},{9,11},{10,... | collective-permute-start | bytes 3932168 | tf_op jit(solution)/shard_map/cond/branch_0_fun/ppermute | solution.py:438
  87.8 32.3 %collective-permute-start.9 = (bf16[2560,256]{1,0:T(8,128)(2,1)S(1)}, bf16[2560,256]{1,0:T(8,128)(2,1)S(1)}, u32[]{:S(2)}, u32[]{:S(2)}) collective-permute-start(bf16[2560,256]{1,0:T(8,128)(2,1)S(1)} %bitcast.28), channel_id=1, source_target_pairs={{0,1},{1,2},{2,3},{3,0},{4,5},{5,6},{6,7},{7,4},{8,9},{9,10},{10,1... | collective-permute-start | bytes 3932168 | tf_op jit(solution)/shard_map/cond/branch_0_fun/ppermute | solution.py:438
  88.6 6.3 %collective-permute-start.13 = (f32[64,512]{1,0:T(8,128)S(1)}, f32[64,512]{1,0:T(8,128)S(1)}, u32[]{:S(2)}, u32[]{:S(2)}) collective-permute-start(f32[64,512]{1,0:T(8,128)S(1)} %get-tuple-element.59.refs_6_), channel_id=1, source_target_pairs={{0,32},{16,48},{32,64},{48,80},{64,96},{80,112},{96,0},{112,16},{1... | collective-permute-start | bytes 393224 | tf_op jit(solution)/shard_map/cond/branch_0_fun/ppermute | solution.py:72
  93.9 5.9 %collective-permute-start.14 = (f32[64,512]{1,0:T(8,128)S(1)}, f32[64,512]{1,0:T(8,128)S(1)}, u32[]{:S(2)}, u32[]{:S(2)}) collective-permute-start(f32[64,512]{1,0:T(8,128)S(1)} %get-tuple-element.59.refs_6_), channel_id=1, source_target_pairs={{0,48},{16,64},{32,80},{48,96},{64,112},{80,0},{96,16},{112,32},{1... | collective-permute-start | bytes 393224 | tf_op jit(solution)/shard_map/cond/branch_0_fun/ppermute | solution.py:72
  95.0 7.4 %collective-permute-start.15 = (f32[64,512]{1,0:T(8,128)S(1)}, f32[64,512]{1,0:T(8,128)S(1)}, u32[]{:S(2)}, u32[]{:S(2)}) collective-permute-start(f32[64,512]{1,0:T(8,128)S(1)} %get-tuple-element.59.refs_6_), channel_id=1, source_target_pairs={{0,64},{16,80},{32,96},{48,112},{64,0},{80,16},{96,32},{112,48},{1... | collective-permute-start | bytes 393224 | tf_op jit(solution)/shard_map/cond/branch_0_fun/ppermute | solution.py:72
  99.8 5.9 %collective-permute-start.16 = (f32[64,512]{1,0:T(8,128)S(1)}, f32[64,512]{1,0:T(8,128)S(1)}, u32[]{:S(2)}, u32[]{:S(2)}) collective-permute-start(f32[64,512]{1,0:T(8,128)S(1)} %get-tuple-element.59.refs_6_), channel_id=1, source_target_pairs={{0,80},{16,96},{32,112},{48,0},{64,16},{80,32},{96,48},{112,64},{1... | collective-permute-start | bytes 393224 | tf_op jit(solution)/shard_map/cond/branch_0_fun/ppermute | solution.py:72
  102.4 7.5 %collective-permute-start.17 = (f32[64,512]{1,0:T(8,128)S(1)}, f32[64,512]{1,0:T(8,128)S(1)}, u32[]{:S(2)}, u32[]{:S(2)}) collective-permute-start(f32[64,512]{1,0:T(8,128)S(1)} %get-tuple-element.59.refs_6_), channel_id=1, source_target_pairs={{0,96},{16,112},{32,0},{48,16},{64,32},{80,48},{96,64},{112,80},{1... | collective-permute-start | bytes 393224 | tf_op jit(solution)/shard_map/cond/branch_0_fun/ppermute | solution.py:72
  147.1 11.1 %all-to-all-start.1 = ((f32[16,6,128]{2,1,0:T(8,128)}), f32[16,6,128]{2,1,0:T(8,128)S(1)}, u32[]{:S(2)}, u32[]{:S(2)}) async-start(f32[16,6,128]{2,1,0:T(8,128)} %broadcast_in_dim_broadcast_in_dim_broadcast_in_dim.2), calls=%async_computation.1 | async-start | bytes 131072 | tf_op jit(solution)/shard_map/all_to_all | solution.py:466
  (9 other events, 225.1 us)
